TPU v7x, 128 devices: a whole 4x4x4 slice. The times are simulated.
128 devices in a mesh: outer: 32 (over z, y, core), grp: 4 (over x).
Axes of the slice: x: 4, y: 4, z: 4, core: 2. Of those that a mesh axis runs over, the one named last changes fastest.
Arguments:
- link_ids: int32 [98304, 8], P(('outer', 'grp')), may hold values from 0 to 98303, as said below
- path_states: bfloat16 [98304, 8, 128], P(('outer', 'grp')), may hold values from -1 to 1
- final_grad: bfloat16 [98304, 128], P(('outer', 'grp')), may hold values from -6 to 6
- link_states: bfloat16 [98304, 128], P(('outer', 'grp')), may hold values from -6 to 6
- agg_grad: bfloat16 [98304, 128], P(('outer', 'grp')), may hold values from -3 to 3
- w_in: bfloat16 [128, 384], replicated, may hold values from -0.5 to 0.5
- w_rec: bfloat16 [128, 384], replicated, may hold values from -0.5 to 0.5
- b_in: float32 [384], replicated, may hold values from -1 to 1
- b_rec: float32 [384], replicated, may hold values from -1 to 1
Outputs:
- path_grad: bfloat16 [98304, 128], P(('outer', 'grp'))
- link_grad: float32 [98304, 128], P(('outer', 'grp'))
- w_in_grad: float32 [128, 384], replicated
- w_rec_grad: float32 [128, 384], replicated
- b_in_grad: float32 [384], replicated
- b_rec_grad: float32 [384], replicated
Inputs may be any that keep to these rules, and one draw needn't show every extreme that they name: `link_ids`: within the 6144 hops of each device's paths (aligned blocks), at most 72 lie on links of any one owner (owner = id // 768), and exactly 72 for some owner in every block.
All inputs are finite; a program needn't handle non-finite values.
Results may differ from a plain program's by a relative error of at most 0.0035.
Values may be sent and summed in bfloat16 or wider, within the bound.
A program may use at most 128 MiB of HBM per device.

v0:
```python
import math
import jax
import jax.numpy as jnp
from jax import lax
from jax.sharding import PartitionSpec as P


def gru_backward(carry_grad, inputs, states, w_in, w_rec, b_in, b_rec):
    width = states.shape[-1]
    from_input = jnp.dot(inputs, w_in, preferred_element_type=jnp.float32) + b_in
    from_state = jnp.dot(states, w_rec, preferred_element_type=jnp.float32) + b_rec
    update_gate = jax.nn.sigmoid(from_input[:, :width] + from_state[:, :width])
    reset_gate = jax.nn.sigmoid(from_input[:, width : 2 * width] + from_state[:, width : 2 * width])
    recur_part = from_state[:, 2 * width :]
    candidate = jnp.tanh(from_input[:, 2 * width :] + reset_gate * recur_part)
    state_wide = states.astype(jnp.float32)
    cand_pre = carry_grad * (1.0 - update_gate) * (1.0 - candidate * candidate)
    update_pre = carry_grad * (state_wide - candidate) * update_gate * (1.0 - update_gate)
    reset_pre = cand_pre * recur_part * reset_gate * (1.0 - reset_gate)
    input_pre = jnp.concatenate([update_pre, reset_pre, cand_pre], axis=1).astype(jnp.bfloat16)
    state_pre = jnp.concatenate([update_pre, reset_pre, cand_pre * reset_gate], axis=1).astype(
        jnp.bfloat16
    )
    input_grad = jnp.dot(input_pre, w_in.T, preferred_element_type=jnp.float32)
    state_grad = carry_grad * update_gate + jnp.dot(
        state_pre, w_rec.T, preferred_element_type=jnp.float32
    )
    w_in_term = jnp.dot(inputs.T, input_pre, preferred_element_type=jnp.float32)
    w_rec_term = jnp.dot(states.T, state_pre, preferred_element_type=jnp.float32)
    b_in_term = jnp.sum(input_pre.astype(jnp.float32), axis=0)
    b_rec_term = jnp.sum(state_pre.astype(jnp.float32), axis=0)
    return (state_grad, input_grad, w_in_term, w_rec_term, b_in_term, b_rec_term)


def per_device(link_ids, path_states, final_grad, link_states, agg_grad, w_in, w_rec, b_in, b_rec):
    path_count, hop_count = link_ids.shape
    width = link_states.shape[1]
    row_count = path_count * hop_count
    devices = lax.axis_size(("outer", "grp"))
    capacity = 3 * row_count // (2 * devices)
    links_dev = link_states.shape[0]
    flat_ids = jnp.transpose(link_ids).reshape(row_count)
    owners = flat_ids // links_dev
    local_ids = flat_ids - owners * links_dev
    by_owner = jnp.argsort(owners, stable=True)
    sorted_owners = owners[by_owner]
    group_starts = jnp.searchsorted(
        sorted_owners, jnp.arange(devices, dtype=jnp.int32), side="left"
    )
    slot_sorted = (
        sorted_owners * capacity
        + jnp.arange(row_count, dtype=jnp.int32)
        - group_starts[sorted_owners]
    )
    slots = jnp.zeros((row_count,), jnp.int32).at[by_owner].set(slot_sorted)
    requests = jnp.full((devices * capacity,), links_dev, jnp.int32).at[slots].set(local_ids)
    requests = requests.reshape(devices, capacity)
    link_table = jnp.concatenate([link_states, agg_grad], axis=1)
    asked_ids = lax.all_to_all(requests, ("outer", "grp"), split_axis=0, concat_axis=0, tiled=True)
    clipped = jnp.minimum(asked_ids, links_dev - 1)
    returned = lax.all_to_all(
        link_table[clipped], ("outer", "grp"), split_axis=0, concat_axis=0, tiled=True
    )
    fetched = returned.reshape(devices * capacity, 2 * width)[slots].reshape(
        hop_count, path_count, 2 * width
    )
    carry_grad = final_grad.astype(jnp.float32)
    w_in_sum = jnp.zeros(w_in.shape, jnp.float32)
    w_rec_sum = jnp.zeros(w_rec.shape, jnp.float32)
    b_in_sum = jnp.zeros(b_in.shape, jnp.float32)
    b_rec_sum = jnp.zeros(b_rec.shape, jnp.float32)
    hop_grads = [None] * hop_count
    for hop in range(hop_count - 1, -1, -1):
        hop_rows = fetched[hop]
        carry_grad = carry_grad + hop_rows[:, width:].astype(jnp.float32)
        carry_grad, input_grad, w_in_term, w_rec_term, b_in_term, b_rec_term = gru_backward(
            carry_grad, hop_rows[:, :width], path_states[:, hop], w_in, w_rec, b_in, b_rec
        )
        hop_grads[hop] = input_grad
        w_in_sum = w_in_sum + w_in_term
        w_rec_sum = w_rec_sum + w_rec_term
        b_in_sum = b_in_sum + b_in_term
        b_rec_sum = b_rec_sum + b_rec_term
    grad_rows_all = jnp.stack(hop_grads, axis=0).reshape(row_count, width)
    outgoing = jnp.zeros((devices * capacity, width), jnp.float32).at[slots].set(grad_rows_all)
    incoming = lax.all_to_all(
        outgoing.reshape(devices, capacity, width).astype(jnp.bfloat16),
        ("outer", "grp"),
        split_axis=0,
        concat_axis=0,
        tiled=True,
    ).astype(jnp.float32)
    link_grad = (
        jnp.zeros((links_dev, width), jnp.float32)
        .at[asked_ids.reshape(-1)]
        .add(incoming.reshape(devices * capacity, width), mode="drop")
    )
    w_in_all, w_rec_all, b_in_all, b_rec_all = lax.psum(
        (w_in_sum, w_rec_sum, b_in_sum, b_rec_sum), ("outer", "grp")
    )
    norm_scale = 1.0 / math.sqrt(row_count * devices)
    return (
        carry_grad.astype(jnp.bfloat16),
        link_grad,
        w_in_all * norm_scale,
        w_rec_all * norm_scale,
        b_in_all * norm_scale,
        b_rec_all * norm_scale,
    )


def solution(mesh):
    placed = (
        P(("outer", "grp"), None),
        P(("outer", "grp"), None, None),
        P(("outer", "grp"), None),
        P(("outer", "grp"), None),
        P(("outer", "grp"), None),
        P(),
        P(),
        P(),
        P(),
    )
    return jax.shard_map(
        per_device,
        mesh=mesh,
        in_specs=placed,
        out_specs=(P(("outer", "grp"), None), P(("outer", "grp"), None), P(), P(), P(), P()),
        check_vma=False,
    )
```

profile of v0, /device:TPU:1, one launch (start us, length us, event | category | flops | bytes accessed | tf_op | source)
XLA Modules:
  0.0 602.4 jit_solution(14700198796793534372)
XLA Ops:
  8.0 6.7 %sort.17 = (s32[6144]{0:T(1024)}, s32[6144]{0:T(1024)S(1)}) sort(s32[6144]{0:T(1024)S(1)} %get-tuple-element.208, s32[6144]{0:T(1024)S(1)} %iota.10), dimensions={0}, to_apply=%region_0.1 | sort | flops 79872 | bytes 98304 | tf_op jit(solution)/shard_map/jit(argsort)/sort | solution.py:45
  14.8 34.3 %gather_fusion.1 = s32[6144]{0:T(1024)S(1)} fusion(s32[6144]{0:T(1024)S(1)} %get-tuple-element.208, s32[6144]{0:T(1024)S(1)} %get-tuple-element.209), kind=kCustom, calls=%fused_computation.1 | custom fusion | bytes 73728 | tf_op jit(solution)/shard_map/gather | solution.py:46
  49.1 15.8 %while.24 = (s32[]{:T(128)}, u32[128]{0:T(128)S(1)}, u32[128]{0:T(128)S(1)}, s32[6144]{0:T(1024)S(1)}, s32[]{:T(128)}, /*index=5*/s32[]{:T(128)}, s32[]{}) while((s32[]{:T(128)}, u32[128]{0:T(128)S(1)}, u32[128]{0:T(128)S(1)}, s32[6144]{0:T(1024)S(1)}, s32[]{:T(128)}, /*index=5*/s32[]{:T(128)}, s32[]{}) %tuple.107), condition=%wide.region_2.3_spmd.clone, body=%wide.region_1.2_spmd.clone.sunk | while | flops 2692 | bytes 10340 | solution.py:47
  65.0 36.8 %gather_fusion.2 = s32[6144]{0:T(1024)S(1)} fusion(s32[128]{0:T(128)S(1)} %convert_element_type.136, s32[6144]{0:T(1024)S(1)} %broadcast_clamp_fusion.2), kind=kCustom, calls=%fused_computation.2 | custom fusion | bytes 73728 | tf_op jit(solution)/shard_map/gather | solution.py:53
  101.8 23.0 %scatter_custom_fusion = s32[6144]{0:T(1024)S(1)} fusion(s32[6144]{0:T(1024)S(1)} %get-tuple-element.210, s32[6144]{0:T(1024)S(1)} %add_subtract_fusion, s32[]{:T(128)} %constant.53.clone.1), kind=kCustom, calls=%fused_computation.309 | custom fusion | bytes 24580 | tf_op jit(solution)/shard_map/scatter | solution.py:55
  125.4 23.0 %scatter_custom_fusion.1 = s32[9216]{0:T(1024)S(1)} fusion(s32[6144]{0:T(1024)S(1)} %get-tuple-element.206, s32[6144]{0:T(1024)S(1)} %get-tuple-element.207, s32[]{:T(128)} %constant.52.clone.1), kind=kCustom, calls=%fused_computation.304 | custom fusion | bytes 36868 | tf_op jit(solution)/shard_map/scatter | solution.py:56
  149.1 11.5 %all-to-all-start = ((s32[128,1,72]{2,1,0:T(1,128)}), s32[128,1,72]{2,1,0:T(1,128)S(1)}, u32[]{:S(2)}, u32[]{:S(2)}) async-start(s32[128,1,72]{2,1,0:T(1,128)} %bitcast.3), calls=%async_computation | async-start | bytes 131072 | tf_op jit(solution)/shard_map/all_to_all | solution.py:59
  160.7 9.5 %all-to-all-done = s32[128,1,72]{2,1,0:T(1,128)S(1)} async-done(((s32[128,1,72]{2,1,0:T(1,128)}), s32[128,1,72]{2,1,0:T(1,128)S(1)}, u32[]{:S(2)}, u32[]{:S(2)}) %all-to-all-start) | async-done | bytes 36896 | tf_op jit(solution)/shard_map/all_to_all | solution.py:59
  172.4 36.9 %gather_fusion.3 = bf16[9216,256]{1,0:T(8,128)(2,1)} fusion(bf16[768,256]{1,0:T(8,128)(2,1)S(1)} %pad_maximum_fusion.24, s32[9216]{0:T(1024)S(1)} %broadcast_clamp_fusion), kind=kCustom, calls=%fused_computation.3 | custom fusion | bytes 9474048 | tf_op jit(solution)/shard_map/gather | solution.py:62
  209.3 6.0 all-to-all-start.1
  215.3 3.3 fusion.154
  236.4 37.7 %all-to-all-done.1 = bf16[128,72,256]{2,1,0:T(8,128)(2,1)} async-done(((bf16[128,72,256]{2,1,0:T(8,128)(2,1)}), bf16[128,72,256]{2,1,0:T(8,128)(2,1)}, u32[]{:S(2)}, u32[]{:S(2)}) %all-to-all-start.1) | async-done | bytes 4718624 | tf_op jit(solution)/shard_map/all_to_all | solution.py:61
  274.1 25.2 %gather_fusion.4 = bf16[6144,256]{1,0:T(8,128)(2,1)S(1)} fusion(bf16[9216,256]{1,0:T(8,128)(2,1)} %bitcast.6, s32[6144]{0:T(1024)} %get-tuple-element.205), kind=kCustom, calls=%fused_computation.4 | custom fusion | bytes 6316032 | tf_op jit(solution)/shard_map/gather | solution.py:64
  315.3 1.8 copy.110
  317.1 1.8 copy.112
  325.8 2.1 fusion.137
  357.3 18.5 %scatter_custom_fusion.2 = f32[9216,128]{1,0:T(8,128)} fusion(s32[6144]{0:T(1024)} %copy-done.119, f32[6144,128]{1,0:T(8,128)} %bitcast.135, f32[]{:T(128)} %constant.64.clone.1), kind=kCustom, calls=%fused_computation.19 | custom fusion | bytes 4719104 | tf_op jit(solution)/shard_map/scatter | solution.py:85
  375.8 3.5 convert_element_type.154
  379.3 5.2 all-to-all-start.2
  384.6 1.7 copy.96
  395.5 74.0 %all-reduce = (f32[384]{0:T(512)S(1)}, f32[384]{0:T(512)S(1)}) all-reduce(f32[384]{0:T(512)S(1)} %get-tuple-element.221, f32[384]{0:T(512)S(1)} %get-tuple-element.220), channel_id=1, replica_groups=mesh['outer'=32,'grp'=4] {'outer','grp'}, use_global_device_ids=true, to_apply=%region_17.18 | all-reduce | flops 768 | bytes 6144 | tf_op jit(solution)/shard_map/psum | solution.py:98
  470.6 72.1 %all-reduce.4.cloned.1.call-done = (f32[128,384]{1,0:T(8,128)}, f32[128,384]{1,0:T(8,128)}) async-done(((f32[128,384]{1,0:T(8,128)}, f32[128,384]{1,0:T(8,128)}), (f32[128,384]{1,0:T(8,128)}, f32[128,384]{1,0:T(8,128)})) %all-reduce.4.cloned.1.call-update) | async-done | bytes 393232 | tf_op jit(solution)/shard_map/psum | solution.py:98
  542.8 1.8 broadcast_multiply_fusion
  544.6 50.7 %scatter_custom_fusion.3 = f32[768,128]{1,0:T(8,128)} fusion(s32[9216]{0:T(1024)} %bitcast.133, bf16[9216,128]{1,0:T(8,128)(2,1)} %bitcast.28, f32[]{:T(128)} %constant.64.clone.1), kind=kCustom, calls=%fused_computation.17 | custom fusion | flops 2359296 | bytes 2753024 | tf_op jit(solution)/shard_map/scatter-add | solution.py:96
  (400 shorter events, 98.7 us)
Async XLA Ops:
  7.2 293.4 %copy-start = (bf16[128,384]{1,0:T(8,128)(2,1)S(1)}, bf16[128,384]{1,0:T(8,128)(2,1)}, u32[]{:S(2)}) copy-start(bf16[128,384]{1,0:T(8,128)(2,1)} %param.16) | copy-start | bytes 294916
  64.9 95.7 %copy-start.99 = (bf16[768,128]{1,0:T(8,128)(2,1)S(1)}, bf16[768,128]{1,0:T(8,128)(2,1)}, u32[]{:S(2)}) copy-start(bf16[768,128]{1,0:T(8,128)(2,1)} %param.15) | copy-start | bytes 589828
  65.0 95.7 %copy-start.100 = (bf16[768,128]{1,0:T(8,128)(2,1)S(1)}, bf16[768,128]{1,0:T(8,128)(2,1)}, u32[]{:S(2)}) copy-start(bf16[768,128]{1,0:T(8,128)(2,1)} %param.14) | copy-start | bytes 589828
  125.4 23.7 %copy-start.119 = (s32[6144]{0:T(1024)}, s32[6144]{0:T(1024)S(1)}, u32[]{:S(2)}) copy-start(s32[6144]{0:T(1024)S(1)} %get-tuple-element.206) | copy-start | bytes 73732
  149.1 21.1 %all-to-all-start = ((s32[128,1,72]{2,1,0:T(1,128)}), s32[128,1,72]{2,1,0:T(1,128)S(1)}, u32[]{:S(2)}, u32[]{:S(2)}) async-start(s32[128,1,72]{2,1,0:T(1,128)} %bitcast.3), calls=%async_computation | async-start | bytes 131072 | tf_op jit(solution)/shard_map/all_to_all | solution.py:59
  209.3 64.8 %all-to-all-start.1 = ((bf16[128,72,256]{2,1,0:T(8,128)(2,1)}), bf16[128,72,256]{2,1,0:T(8,128)(2,1)}, u32[]{:S(2)}, u32[]{:S(2)}) async-start(bf16[128,72,256]{2,1,0:T(8,128)(2,1)} %bitcast.129), calls=%async_computation.1 | async-start | bytes 9437184 | tf_op jit(solution)/shard_map/all_to_all | solution.py:61
  327.9 27.3 %copy-start.38 = (bf16[768,128]{0,1:T(8,128)(2,1)}, bf16[768,128]{0,1:T(8,128)(2,1)S(1)}, u32[]{:S(2)}) copy-start(bf16[768,128]{0,1:T(8,128)(2,1)S(1)} %get-tuple-element.137) | copy-start | bytes 589828
  328.6 26.6 %copy-start.40 = (bf16[768,128]{0,1:T(8,128)(2,1)}, bf16[768,128]{0,1:T(8,128)(2,1)S(1)}, u32[]{:S(2)}) copy-start(bf16[768,128]{0,1:T(8,128)(2,1)S(1)} %get-tuple-element.193) | copy-start | bytes 589828
  328.6 26.6 %copy-start.42 = (bf16[768,128]{0,1:T(8,128)(2,1)}, bf16[768,128]{0,1:T(8,128)(2,1)S(1)}, u32[]{:S(2)}) copy-start(bf16[768,128]{0,1:T(8,128)(2,1)S(1)} %get-tuple-element.194) | copy-start | bytes 589828
  331.2 23.6 %copy-start.101 = (bf16[768,128]{0,1:T(8,128)(2,1)}, bf16[768,128]{0,1:T(8,128)(2,1)S(1)}, u32[]{:S(2)}) copy-start(bf16[768,128]{0,1:T(8,128)(2,1)S(1)} %get-tuple-element.140) | copy-start | bytes 589828
  331.5 23.3 %copy-start.46 = (bf16[768,128]{0,1:T(8,128)(2,1)}, bf16[768,128]{0,1:T(8,128)(2,1)S(1)}, u32[]{:S(2)}) copy-start(bf16[768,128]{0,1:T(8,128)(2,1)S(1)} %get-tuple-element.191) | copy-start | bytes 589828
  331.5 23.3 %copy-start.47 = (bf16[768,128]{0,1:T(8,128)(2,1)}, bf16[768,128]{0,1:T(8,128)(2,1)S(1)}, u32[]{:S(2)}) copy-start(bf16[768,128]{0,1:T(8,128)(2,1)S(1)} %get-tuple-element.192) | copy-start | bytes 589828
  333.6 20.7 %copy-start.102 = (bf16[768,128]{0,1:T(8,128)(2,1)}, bf16[768,128]{0,1:T(8,128)(2,1)S(1)}, u32[]{:S(2)}) copy-start(bf16[768,128]{0,1:T(8,128)(2,1)S(1)} %get-tuple-element.143) | copy-start | bytes 589828
  334.3 20.0 %copy-start.49 = (bf16[768,128]{0,1:T(8,128)(2,1)}, bf16[768,128]{0,1:T(8,128)(2,1)S(1)}, u32[]{:S(2)}) copy-start(bf16[768,128]{0,1:T(8,128)(2,1)S(1)} %get-tuple-element.189) | copy-start | bytes 589828
  334.3 20.0 %copy-start.51 = (bf16[768,128]{0,1:T(8,128)(2,1)}, bf16[768,128]{0,1:T(8,128)(2,1)S(1)}, u32[]{:S(2)}) copy-start(bf16[768,128]{0,1:T(8,128)(2,1)S(1)} %get-tuple-element.190) | copy-start | bytes 589828
  336.4 17.5 %copy-start.104 = (bf16[768,128]{0,1:T(8,128)(2,1)}, bf16[768,128]{0,1:T(8,128)(2,1)S(1)}, u32[]{:S(2)}) copy-start(bf16[768,128]{0,1:T(8,128)(2,1)S(1)} %get-tuple-element.146) | copy-start | bytes 589828
  337.1 16.8 %copy-start.55 = (bf16[768,128]{0,1:T(8,128)(2,1)}, bf16[768,128]{0,1:T(8,128)(2,1)S(1)}, u32[]{:S(2)}) copy-start(bf16[768,128]{0,1:T(8,128)(2,1)S(1)} %get-tuple-element.187) | copy-start | bytes 589828
  337.1 16.8 %copy-start.57 = (bf16[768,128]{0,1:T(8,128)(2,1)}, bf16[768,128]{0,1:T(8,128)(2,1)S(1)}, u32[]{:S(2)}) copy-start(bf16[768,128]{0,1:T(8,128)(2,1)S(1)} %get-tuple-element.188) | copy-start | bytes 589828
  339.2 14.3 %copy-start.106 = (bf16[768,128]{0,1:T(8,128)(2,1)}, bf16[768,128]{0,1:T(8,128)(2,1)S(1)}, u32[]{:S(2)}) copy-start(bf16[768,128]{0,1:T(8,128)(2,1)S(1)} %get-tuple-element.149) | copy-start | bytes 589828
  339.9 13.6 %copy-start.63 = (bf16[768,128]{0,1:T(8,128)(2,1)}, bf16[768,128]{0,1:T(8,128)(2,1)S(1)}, u32[]{:S(2)}) copy-start(bf16[768,128]{0,1:T(8,128)(2,1)S(1)} %get-tuple-element.186) | copy-start | bytes 589828
  339.9 46.4 %copy-start.61 = (bf16[768,128]{0,1:T(8,128)(2,1)}, bf16[768,128]{0,1:T(8,128)(2,1)S(1)}, u32[]{:S(2)}) copy-start(bf16[768,128]{0,1:T(8,128)(2,1)S(1)} %get-tuple-element.185) | copy-start | bytes 589828
  342.1 11.1 %copy-start.108 = (bf16[768,128]{0,1:T(8,128)(2,1)}, bf16[768,128]{0,1:T(8,128)(2,1)S(1)}, u32[]{:S(2)}) copy-start(bf16[768,128]{0,1:T(8,128)(2,1)S(1)} %get-tuple-element.152) | copy-start | bytes 589828
  379.3 165.2 %all-to-all-start.2 = ((bf16[128,72,128]{2,1,0:T(8,128)(2,1)}), bf16[128,72,128]{2,1,0:T(8,128)(2,1)}, u32[]{:S(2)}, u32[]{:S(2)}) async-start(bf16[128,72,128]{2,1,0:T(8,128)(2,1)} %bitcast.130), calls=%async_computation.2 | async-start | bytes 4718592 | tf_op jit(solution)/shard_map/all_to_all | solution.py:86
  384.6 158.2 %all-reduce.4.cloned.1.call-start = ((), (), s32[]{:S(2)}) async-start(), calls=%async_computation.3 | async-start | bytes 786432 | tf_op jit(solution)/shard_map/psum | solution.py:98
  (101 other events, 241.1 us)
Sparse Core Ops, SparseCore 0:
  391.4 151.3 all-reduce.3
where the time goes:
time: 610 us; the launch traced here: 602 us
  local copies, waits for them, and re-layouts  257 us (42%)
  waiting for transfers between devices  119 us (20%)
  other arithmetic  74.6 us (12%)
  blocking collectives  74 us (12%)
  matrix products  38.7 us (6%)
  starting transfers between devices  22.7 us (4%)
  between operations  15.9 us (3%)
    psum x1, blocking collectives, per_device(): lax.psum((w_in_sum, w_rec_sum, b_in_sum, b_rec_sum), ('outer', 'grp'))  74 us
    psum x1, waiting for transfers between devices, per_device(): lax.psum((w_in_sum, w_rec_sum, b_in_sum, b_rec_sum), ('outer', 'grp'))  72.1 us
    scatter-add x1, other arithmetic, per_device(): link_grad = jnp.zeros((links_dev, width), jnp.float32).at[asked_ids.resha...  50.7 us
    all_to_all x1, waiting for transfers between devices, per_device(): lax.all_to_all(link_table[clipped], ('outer', 'grp'), split_axis=0, conca...  37.7 us
    unnamed x260, local copies, waits for them, and re-layouts  37.2 us
    gather x1, local copies, waits for them, and re-layouts, per_device(): link_table[clipped]  36.9 us
    gather x1, local copies, waits for them, and re-layouts, per_device(): group_starts[sorted_owners]  36.8 us
    gather x1, local copies, waits for them, and re-layouts, per_device(): sorted_owners = owners[by_owner]  34.3 us
  transfers between devices with their start and end apart: 4, of which 3 were waited for; matrix products, arithmetic and copies ran while one was open for 5% of the time, Pallas kernels for 0%

commit v1 on v0

--- a/solution.py
+++ b/solution.py
@@ -96,7 +96,7 @@
         .add(incoming.reshape(devices * capacity, width), mode="drop")
     )
     w_in_all, w_rec_all, b_in_all, b_rec_all = lax.psum(
-        (w_in_sum, w_rec_sum, b_in_sum, b_rec_sum), ("outer", "grp")
+        lax.psum((w_in_sum, w_rec_sum, b_in_sum, b_rec_sum), "grp"), "outer"
     )
     norm_scale = 1.0 / math.sqrt(row_count * devices)
     return (

time: 610 us -> 651 us (1.067)
  waiting for transfers between devices: 119 us -> 147 us
  blocking collectives: 74 us -> 86.1 us
    psum x1 -> x2, waiting for transfers between devices: 72.1 us -> 100 us  [the longest x1 100 us: per_device(): lax.psum(lax.psum((w_in_sum, w_rec_sum, b_in_sum, b_rec_sum), 'grp'), 'ou...]
    psum x1 -> x2, blocking collectives: 74 us -> 86.1 us  [the longest x1 64.1 us: per_device(): lax.psum(lax.psum((w_in_sum, w_rec_sum, b_in_sum, b_rec_sum), 'grp'), 'ou...]
  transfers between devices with their start and end apart: 4 -> 5, of which waited for: 3 -> 3; matrix products, arithmetic and copies ran while one was open for 5% -> 5% of each run, Pallas kernels for 0% -> 0%
where the time goes in v1:
time: 651 us; the launch traced here: 643 us
  local copies, waits for them, and re-layouts  257 us (39%)
  waiting for transfers between devices  147 us (23%)
  blocking collectives  86.1 us (13%)
  other arithmetic  74.6 us (11%)
  matrix products  38.7 us (6%)
  starting transfers between devices  22.8 us (4%)
  between operations  15.9 us (2%)
    psum x1, waiting for transfers between devices, per_device(): lax.psum(lax.psum((w_in_sum, w_rec_sum, b_in_sum, b_rec_sum), 'grp'), 'ou...  100 us
    psum x1, blocking collectives, per_device(): lax.psum(lax.psum((w_in_sum, w_rec_sum, b_in_sum, b_rec_sum), 'grp'), 'ou...  64.1 us
    scatter-add x1, other arithmetic, per_device(): link_grad = jnp.zeros((links_dev, width), jnp.float32).at[asked_ids.resha...  50.7 us
    all_to_all x1, waiting for transfers between devices, per_device(): lax.all_to_all(link_table[clipped], ('outer', 'grp'), split_axis=0, conca...  37.7 us
    unnamed x260, local copies, waits for them, and re-layouts  37.2 us
    gather x1, local copies, waits for them, and re-layouts, per_device(): link_table[clipped]  36.9 us
    gather x1, local copies, waits for them, and re-layouts, per_device(): group_starts[sorted_owners]  36.8 us
    gather x1, local copies, waits for them, and re-layouts, per_device(): sorted_owners = owners[by_owner]  34.3 us
  transfers between devices with their start and end apart: 5, of which 3 were waited for; matrix products, arithmetic and copies ran while one was open for 5% of the time, Pallas kernels for 0%

profile of v1, /device:TPU:1, one launch (start us, length us, event | category | flops | bytes accessed | tf_op | source)
XLA Modules:
  0.0 642.6 jit_solution(12628175410985241684)
XLA Ops:
  8.0 6.7 %sort.17 = (s32[6144]{0:T(1024)}, s32[6144]{0:T(1024)S(1)}) sort(s32[6144]{0:T(1024)S(1)} %get-tuple-element.212, s32[6144]{0:T(1024)S(1)} %iota.10), dimensions={0}, to_apply=%region_0.1 | sort | flops 79872 | bytes 98304 | tf_op jit(solution)/shard_map/jit(argsort)/sort | solution.py:45
  14.8 34.3 %gather_fusion.1 = s32[6144]{0:T(1024)S(1)} fusion(s32[6144]{0:T(1024)S(1)} %get-tuple-element.212, s32[6144]{0:T(1024)S(1)} %get-tuple-element.213), kind=kCustom, calls=%fused_computation.1 | custom fusion | bytes 73728 | tf_op jit(solution)/shard_map/gather | solution.py:46
  49.1 15.8 %while.24 = (s32[]{:T(128)}, u32[128]{0:T(128)S(1)}, u32[128]{0:T(128)S(1)}, s32[6144]{0:T(1024)S(1)}, s32[]{:T(128)}, /*index=5*/s32[]{:T(128)}, s32[]{}) while((s32[]{:T(128)}, u32[128]{0:T(128)S(1)}, u32[128]{0:T(128)S(1)}, s32[6144]{0:T(1024)S(1)}, s32[]{:T(128)}, /*index=5*/s32[]{:T(128)}, s32[]{}) %tuple.107), condition=%wide.region_2.3_spmd.clone, body=%wide.region_1.2_spmd.clone.sunk | while | flops 2692 | bytes 10340 | solution.py:47
  65.0 36.8 %gather_fusion.2 = s32[6144]{0:T(1024)S(1)} fusion(s32[128]{0:T(128)S(1)} %convert_element_type.136, s32[6144]{0:T(1024)S(1)} %broadcast_clamp_fusion.2), kind=kCustom, calls=%fused_computation.2 | custom fusion | bytes 73728 | tf_op jit(solution)/shard_map/gather | solution.py:53
  101.8 23.0 %scatter_custom_fusion = s32[6144]{0:T(1024)S(1)} fusion(s32[6144]{0:T(1024)S(1)} %get-tuple-element.214, s32[6144]{0:T(1024)S(1)} %add_subtract_fusion, s32[]{:T(128)} %constant.53.clone.1), kind=kCustom, calls=%fused_computation.309 | custom fusion | bytes 24580 | tf_op jit(solution)/shard_map/scatter | solution.py:55
  125.4 23.0 %scatter_custom_fusion.1 = s32[9216]{0:T(1024)S(1)} fusion(s32[6144]{0:T(1024)S(1)} %get-tuple-element.210, s32[6144]{0:T(1024)S(1)} %get-tuple-element.211, s32[]{:T(128)} %constant.52.clone.1), kind=kCustom, calls=%fused_computation.304 | custom fusion | bytes 36868 | tf_op jit(solution)/shard_map/scatter | solution.py:56
  149.1 11.5 %all-to-all-start = ((s32[128,1,72]{2,1,0:T(1,128)}), s32[128,1,72]{2,1,0:T(1,128)S(1)}, u32[]{:S(2)}, u32[]{:S(2)}) async-start(s32[128,1,72]{2,1,0:T(1,128)} %bitcast.3), calls=%async_computation | async-start | bytes 131072 | tf_op jit(solution)/shard_map/all_to_all | solution.py:59
  160.7 9.5 %all-to-all-done = s32[128,1,72]{2,1,0:T(1,128)S(1)} async-done(((s32[128,1,72]{2,1,0:T(1,128)}), s32[128,1,72]{2,1,0:T(1,128)S(1)}, u32[]{:S(2)}, u32[]{:S(2)}) %all-to-all-start) | async-done | bytes 36896 | tf_op jit(solution)/shard_map/all_to_all | solution.py:59
  172.4 36.9 %gather_fusion.3 = bf16[9216,256]{1,0:T(8,128)(2,1)} fusion(bf16[768,256]{1,0:T(8,128)(2,1)S(1)} %pad_maximum_fusion.24, s32[9216]{0:T(1024)S(1)} %broadcast_clamp_fusion), kind=kCustom, calls=%fused_computation.3 | custom fusion | bytes 9474048 | tf_op jit(solution)/shard_map/gather | solution.py:62
  209.3 6.0 all-to-all-start.1
  215.3 3.3 fusion.154
  236.4 37.7 %all-to-all-done.1 = bf16[128,72,256]{2,1,0:T(8,128)(2,1)} async-done(((bf16[128,72,256]{2,1,0:T(8,128)(2,1)}), bf16[128,72,256]{2,1,0:T(8,128)(2,1)}, u32[]{:S(2)}, u32[]{:S(2)}) %all-to-all-start.1) | async-done | bytes 4718624 | tf_op jit(solution)/shard_map/all_to_all | solution.py:61
  274.1 25.2 %gather_fusion.4 = bf16[6144,256]{1,0:T(8,128)(2,1)S(1)} fusion(bf16[9216,256]{1,0:T(8,128)(2,1)} %bitcast.6, s32[6144]{0:T(1024)} %get-tuple-element.209), kind=kCustom, calls=%fused_computation.4 | custom fusion | bytes 6316032 | tf_op jit(solution)/shard_map/gather | solution.py:64
  315.3 1.8 copy.110
  317.1 1.8 copy.112
  325.8 2.1 fusion.137
  357.3 18.5 %scatter_custom_fusion.2 = f32[9216,128]{1,0:T(8,128)} fusion(s32[6144]{0:T(1024)} %copy-done.119, f32[6144,128]{1,0:T(8,128)} %bitcast.135, f32[]{:T(128)} %constant.64.clone.1), kind=kCustom, calls=%fused_computation.19 | custom fusion | bytes 4719104 | tf_op jit(solution)/shard_map/scatter | solution.py:85
  375.8 3.5 convert_element_type.154
  379.3 5.2 all-to-all-start.2
  395.5 22.0 %all-reduce.2 = (f32[384]{0:T(512)S(1)}, f32[384]{0:T(512)S(1)}) all-reduce(f32[384]{0:T(512)S(1)} %get-tuple-element.225, f32[384]{0:T(512)S(1)} %get-tuple-element.224), channel_id=1, replica_groups=mesh['outer'=32,'grp'=4] {'grp'}, use_global_device_ids=true, to_apply=%region_19.20 | all-reduce | flops 768 | bytes 6144 | tf_op jit(solution)/shard_map/psum | solution.py:99
  417.6 64.1 %all-reduce = (f32[384]{0:T(512)S(1)}, f32[384]{0:T(512)S(1)}) all-reduce(f32[384]{0:T(512)S(1)} %get-tuple-element.137, f32[384]{0:T(512)S(1)} %get-tuple-element.138), channel_id=1, replica_groups=mesh['outer'=32,'grp'=4] {'outer'}, use_global_device_ids=true, to_apply=%region_20.21 | all-reduce | flops 768 | bytes 6144 | tf_op jit(solution)/shard_map/psum | solution.py:98
  482.9 100.1 %all-reduce.7.cloned.1.call-done = (f32[128,384]{1,0:T(8,128)}, f32[128,384]{1,0:T(8,128)}) async-done(((f32[128,384]{1,0:T(8,128)}, f32[128,384]{1,0:T(8,128)}), (f32[128,384]{1,0:T(8,128)}, f32[128,384]{1,0:T(8,128)})) %all-reduce.7.cloned.1.call-update) | async-done | bytes 393232 | tf_op jit(solution)/shard_map/psum | solution.py:98
  583.0 1.8 broadcast_multiply_fusion
  584.8 50.7 %scatter_custom_fusion.3 = f32[768,128]{1,0:T(8,128)} fusion(s32[9216]{0:T(1024)} %bitcast.133, bf16[9216,128]{1,0:T(8,128)(2,1)} %bitcast.28, f32[]{:T(128)} %constant.64.clone.1), kind=kCustom, calls=%fused_computation.17 | custom fusion | flops 2359296 | bytes 2753024 | tf_op jit(solution)/shard_map/scatter-add | solution.py:96
  (404 shorter events, 100.6 us)
Async XLA Ops:
  7.2 293.4 %copy-start = (bf16[128,384]{1,0:T(8,128)(2,1)S(1)}, bf16[128,384]{1,0:T(8,128)(2,1)}, u32[]{:S(2)}) copy-start(bf16[128,384]{1,0:T(8,128)(2,1)} %param.16) | copy-start | bytes 294916
  64.9 95.7 %copy-start.99 = (bf16[768,128]{1,0:T(8,128)(2,1)S(1)}, bf16[768,128]{1,0:T(8,128)(2,1)}, u32[]{:S(2)}) copy-start(bf16[768,128]{1,0:T(8,128)(2,1)} %param.15) | copy-start | bytes 589828
  65.0 95.7 %copy-start.100 = (bf16[768,128]{1,0:T(8,128)(2,1)S(1)}, bf16[768,128]{1,0:T(8,128)(2,1)}, u32[]{:S(2)}) copy-start(bf16[768,128]{1,0:T(8,128)(2,1)} %param.14) | copy-start | bytes 589828
  125.4 23.7 %copy-start.119 = (s32[6144]{0:T(1024)}, s32[6144]{0:T(1024)S(1)}, u32[]{:S(2)}) copy-start(s32[6144]{0:T(1024)S(1)} %get-tuple-element.210) | copy-start | bytes 73732
  149.1 21.1 %all-to-all-start = ((s32[128,1,72]{2,1,0:T(1,128)}), s32[128,1,72]{2,1,0:T(1,128)S(1)}, u32[]{:S(2)}, u32[]{:S(2)}) async-start(s32[128,1,72]{2,1,0:T(1,128)} %bitcast.3), calls=%async_computation | async-start | bytes 131072 | tf_op jit(solution)/shard_map/all_to_all | solution.py:59
  209.3 64.8 %all-to-all-start.1 = ((bf16[128,72,256]{2,1,0:T(8,128)(2,1)}), bf16[128,72,256]{2,1,0:T(8,128)(2,1)}, u32[]{:S(2)}, u32[]{:S(2)}) async-start(bf16[128,72,256]{2,1,0:T(8,128)(2,1)} %bitcast.129), calls=%async_computation.1 | async-start | bytes 9437184 | tf_op jit(solution)/shard_map/all_to_all | solution.py:61
  327.9 27.3 %copy-start.38 = (bf16[768,128]{0,1:T(8,128)(2,1)}, bf16[768,128]{0,1:T(8,128)(2,1)S(1)}, u32[]{:S(2)}) copy-start(bf16[768,128]{0,1:T(8,128)(2,1)S(1)} %get-tuple-element.141) | copy-start | bytes 589828
  328.6 26.6 %copy-start.40 = (bf16[768,128]{0,1:T(8,128)(2,1)}, bf16[768,128]{0,1:T(8,128)(2,1)S(1)}, u32[]{:S(2)}) copy-start(bf16[768,128]{0,1:T(8,128)(2,1)S(1)} %get-tuple-element.197) | copy-start | bytes 589828
  328.6 26.6 %copy-start.42 = (bf16[768,128]{0,1:T(8,128)(2,1)}, bf16[768,128]{0,1:T(8,128)(2,1)S(1)}, u32[]{:S(2)}) copy-start(bf16[768,128]{0,1:T(8,128)(2,1)S(1)} %get-tuple-element.198) | copy-start | bytes 589828
  331.2 23.6 %copy-start.101 = (bf16[768,128]{0,1:T(8,128)(2,1)}, bf16[768,128]{0,1:T(8,128)(2,1)S(1)}, u32[]{:S(2)}) copy-start(bf16[768,128]{0,1:T(8,128)(2,1)S(1)} %get-tuple-element.144) | copy-start | bytes 589828
  331.5 23.3 %copy-start.46 = (bf16[768,128]{0,1:T(8,128)(2,1)}, bf16[768,128]{0,1:T(8,128)(2,1)S(1)}, u32[]{:S(2)}) copy-start(bf16[768,128]{0,1:T(8,128)(2,1)S(1)} %get-tuple-element.195) | copy-start | bytes 589828
  331.5 23.3 %copy-start.47 = (bf16[768,128]{0,1:T(8,128)(2,1)}, bf16[768,128]{0,1:T(8,128)(2,1)S(1)}, u32[]{:S(2)}) copy-start(bf16[768,128]{0,1:T(8,128)(2,1)S(1)} %get-tuple-element.196) | copy-start | bytes 589828
  333.6 20.7 %copy-start.102 = (bf16[768,128]{0,1:T(8,128)(2,1)}, bf16[768,128]{0,1:T(8,128)(2,1)S(1)}, u32[]{:S(2)}) copy-start(bf16[768,128]{0,1:T(8,128)(2,1)S(1)} %get-tuple-element.147) | copy-start | bytes 589828
  334.3 20.0 %copy-start.49 = (bf16[768,128]{0,1:T(8,128)(2,1)}, bf16[768,128]{0,1:T(8,128)(2,1)S(1)}, u32[]{:S(2)}) copy-start(bf16[768,128]{0,1:T(8,128)(2,1)S(1)} %get-tuple-element.193) | copy-start | bytes 589828
  334.3 20.0 %copy-start.51 = (bf16[768,128]{0,1:T(8,128)(2,1)}, bf16[768,128]{0,1:T(8,128)(2,1)S(1)}, u32[]{:S(2)}) copy-start(bf16[768,128]{0,1:T(8,128)(2,1)S(1)} %get-tuple-element.194) | copy-start | bytes 589828
  336.4 17.5 %copy-start.104 = (bf16[768,128]{0,1:T(8,128)(2,1)}, bf16[768,128]{0,1:T(8,128)(2,1)S(1)}, u32[]{:S(2)}) copy-start(bf16[768,128]{0,1:T(8,128)(2,1)S(1)} %get-tuple-element.150) | copy-start | bytes 589828
  337.1 16.8 %copy-start.55 = (bf16[768,128]{0,1:T(8,128)(2,1)}, bf16[768,128]{0,1:T(8,128)(2,1)S(1)}, u32[]{:S(2)}) copy-start(bf16[768,128]{0,1:T(8,128)(2,1)S(1)} %get-tuple-element.191) | copy-start | bytes 589828
  337.1 16.8 %copy-start.57 = (bf16[768,128]{0,1:T(8,128)(2,1)}, bf16[768,128]{0,1:T(8,128)(2,1)S(1)}, u32[]{:S(2)}) copy-start(bf16[768,128]{0,1:T(8,128)(2,1)S(1)} %get-tuple-element.192) | copy-start | bytes 589828
  339.2 14.3 %copy-start.106 = (bf16[768,128]{0,1:T(8,128)(2,1)}, bf16[768,128]{0,1:T(8,128)(2,1)S(1)}, u32[]{:S(2)}) copy-start(bf16[768,128]{0,1:T(8,128)(2,1)S(1)} %get-tuple-element.153) | copy-start | bytes 589828
  339.9 13.6 %copy-start.63 = (bf16[768,128]{0,1:T(8,128)(2,1)}, bf16[768,128]{0,1:T(8,128)(2,1)S(1)}, u32[]{:S(2)}) copy-start(bf16[768,128]{0,1:T(8,128)(2,1)S(1)} %get-tuple-element.190) | copy-start | bytes 589828
  339.9 46.4 %copy-start.61 = (bf16[768,128]{0,1:T(8,128)(2,1)}, bf16[768,128]{0,1:T(8,128)(2,1)S(1)}, u32[]{:S(2)}) copy-start(bf16[768,128]{0,1:T(8,128)(2,1)S(1)} %get-tuple-element.189) | copy-start | bytes 589828
  379.3 205.4 %all-to-all-start.2 = ((bf16[128,72,128]{2,1,0:T(8,128)(2,1)}), bf16[128,72,128]{2,1,0:T(8,128)(2,1)}, u32[]{:S(2)}, u32[]{:S(2)}) async-start(bf16[128,72,128]{2,1,0:T(8,128)(2,1)} %bitcast.130), calls=%async_computation.2 | async-start | bytes 4718592 | tf_op jit(solution)/shard_map/all_to_all | solution.py:86
  384.6 97.7 %all-reduce.9.cloned.1.call-start = ((), (), s32[]{:S(2)}) async-start(), calls=%async_computation.4 | async-start | bytes 786432 | tf_op jit(solution)/shard_map/psum | solution.py:99
  391.3 191.7 %all-reduce.7.cloned.1.call-start = ((), (), s32[]{:S(2)}) async-start(), calls=%async_computation.3 | async-start | bytes 786432 | tf_op jit(solution)/shard_map/psum | solution.py:98
  (102 other events, 253.0 us)
Sparse Core Ops, SparseCore 0:
  391.4 45.0 all-reduce.8
  482.4 100.5 all-reduce.6
